TPU v7x, 256 devices: a whole 4x4x8 slice. The times are simulated.
256 devices in a mesh: ctx: 32 (over z, x), head: 8 (over y, core).
Axes of the slice: x: 4, y: 4, z: 8, core: 2. Of those that a mesh axis runs over, the one named last changes fastest.
Arguments:
- queries: bfloat16 [256, 128, 192], P('ctx', 'head'), may hold values from -135 to 135
- absorb_k: bfloat16 [128, 128, 512], P('head'), may hold values from -0.5 to 0.5
- absorb_v: bfloat16 [128, 512, 128], P('head'), may hold values from -1.5 to 1.5
- cache: bfloat16 [32768, 576], P(('ctx', 'head')), may hold values from -4 to 4
- new_entries: bfloat16 [256, 576], P('ctx'), may hold values from -5 to 5
- cache_len: int32 [1], replicated, may hold values from 16384 to 32768
Outputs:
- attended: bfloat16 [256, 128, 128], P('ctx', 'head')
All inputs are finite; a program needn't handle non-finite values.
Results may differ from a plain program's by a relative error of at most 0.0077.
Values may be sent and summed in bfloat16 or wider, within the bound.
A program may use at most 128 MiB of HBM per device.

v0:
```python
import math

import jax
import jax.numpy as jnp
from jax import lax
from jax.sharding import PartitionSpec as P

neg_fill = -1e30


def online_update(run_top, run_total, run_acc, scores, is_valid, values):
    masked = jnp.where(is_valid, scores, neg_fill)
    new_top = jnp.maximum(run_top, jnp.max(masked, axis=2))
    weights = jnp.where(is_valid, jnp.exp(scores - new_top[:, :, None]), 0.0)
    rescale = jnp.exp(run_top - new_top)
    run_total = run_total * rescale + jnp.sum(weights, axis=2)
    mixed = jnp.einsum(
        "qhk,kl->qhl", weights.astype(jnp.bfloat16), values, preferred_element_type=jnp.float32
    )
    run_acc = run_acc * rescale[:, :, None] + mixed
    return (new_top, run_total, run_acc)


def project_values(sums, value_proj):
    return jnp.einsum(
        "rhl,hlv->rhv",
        sums,
        value_proj,
        precision=lax.Precision.HIGHEST,
        preferred_element_type=jnp.float32,
    )


def body(queries, absorb_k, absorb_v, cache, new_entries, cache_len):
    ctx_count = lax.axis_size("ctx")
    my_index = lax.axis_index("ctx")
    tok_rows, head_count, qk_width = queries.shape
    nope_width = absorb_k.shape[1]
    latent = absorb_k.shape[2]
    value_proj = absorb_v.astype(jnp.float32)
    score_div = math.sqrt(qk_width)
    lat_q = jnp.einsum(
        "rhn,hnl->rhl", queries[:, :, :nope_width], absorb_k, preferred_element_type=jnp.float32
    ).astype(jnp.bfloat16)
    absorbed = jnp.concatenate([lat_q, queries[:, :, nope_width:]], axis=2)
    local_keys = lax.all_gather(cache, "head", axis=0, tiled=True)
    key_count = local_keys.shape[0]
    key_base = my_index * key_count
    length = cache_len[0]
    block_len = min(512, key_count)
    new_ranks = jnp.arange(tok_rows, dtype=jnp.int32) * ctx_count + my_index
    new_values = new_entries[:, :latent]
    q_piece = lax.all_gather(absorbed, "ctx", axis=0, tiled=True)
    piece_rows = q_piece.shape[0]
    global_rows = jnp.arange(piece_rows, dtype=jnp.int32)
    q_ranks = global_rows % tok_rows * ctx_count + global_rows // tok_rows
    run_top = jnp.full((piece_rows, head_count), neg_fill, jnp.float32)
    run_total = jnp.zeros((piece_rows, head_count), jnp.float32)
    run_acc = jnp.zeros((piece_rows, head_count, latent), jnp.float32)
    for block_no in range(key_count // block_len):
        key_block = local_keys[block_no * block_len : (block_no + 1) * block_len]
        slot_ids = key_base + block_no * block_len + jnp.arange(block_len, dtype=jnp.int32)
        is_valid = (slot_ids < length)[None, None, :]
        scores = (
            jnp.einsum("qhd,kd->qhk", q_piece, key_block, preferred_element_type=jnp.float32)
            / score_div
        )
        run_top, run_total, run_acc = online_update(
            run_top, run_total, run_acc, scores, is_valid, key_block[:, :latent]
        )
    scores = (
        jnp.einsum("qhd,kd->qhk", q_piece, new_entries, preferred_element_type=jnp.float32)
        / score_div
    )
    is_valid = (new_ranks[None, :] <= q_ranks[:, None])[:, None, :]
    run_top, run_total, run_acc = online_update(
        run_top, run_total, run_acc, scores, is_valid, new_values
    )
    best_top = lax.pmax(run_top, "ctx")
    factor = jnp.exp(run_top - best_top)
    sum_acc, sum_total = (
        lax.psum_scatter(run_acc * factor[:, :, None], "ctx", scatter_dimension=0, tiled=True),
        lax.psum_scatter(run_total * factor, "ctx", scatter_dimension=0, tiled=True),
    )
    sum_out = project_values(sum_acc, value_proj)
    return (sum_out / sum_total[:, :, None]).astype(jnp.bfloat16)


def solution(mesh):
    in_specs = (
        P("ctx", "head", None),
        P("head", None, None),
        P("head", None, None),
        P(("ctx", "head"), None),
        P("ctx", None),
        P(),
    )
    out_specs = P("ctx", "head", None)
    return jax.shard_map(body, mesh=mesh, in_specs=in_specs, out_specs=out_specs, check_vma=False)
```

profile of v0, /device:TPU:1, one launch (start us, length us, event | category | flops | bytes accessed | tf_op | source)
XLA Modules:
  0.0 535.1 jit_solution(8010652966746866722)
XLA Ops:
  6.5 0.0 copy-start
  6.5 0.0 all-gather.5.cloned.1.call-start
  6.5 0.7 all-gather.5.cloned.1.call-update
  7.3 0.0 all-gather.3.cloned.1.call-start
  7.3 0.8 slice.23
  8.1 0.8 slice.24
  8.8 0.0 copy-done
  8.9 0.4 fusion.16
  9.2 0.7 pad_maximum_fusion
  9.9 0.0 all-gather.3.cloned.1.call-update
  9.9 0.0 reduce-scatter.3.cloned.1.call-start
  10.7 0.1 broadcast_compare_fusion
  10.7 29.0 %all-gather.5.cloned.1.call-done = bf16[1024,576]{0,1:T(8,128)(2,1)} async-done(((bf16[128,576]{0,1:T(8,128)(2,1)}), bf16[1024,576]{0,1:T(8,128)(2,1)}) %all-gather.5.cloned.1.call-update) | async-done | bytes 1179664 | tf_op jit(solution)/shard_map/all_gather | solution.py:46
  39.8 85.8 %all-gather.3.cloned.1.call-done = bf16[256,16,576]{2,0,1:T(8,128)(2,1)} async-done(((bf16[8,16,576]{2,0,1:T(8,128)(2,1)}), bf16[256,16,576]{2,0,1:T(8,128)(2,1)}) %all-gather.3.cloned.1.call-update) | async-done | bytes 4718608 | tf_op jit(solution)/shard_map/all_gather | solution.py:53
  125.5 0.0 copy-start.3
  125.5 0.0 copy-start.5
  125.5 9.6 %select_reduce_fusion = (f32[256,16]{0,1:T(8,128)S(1)}, f32[256,16,512]{2,0,1:T(8,128)}) fusion(pred[512]{0:T(512)(128)(4,1)S(1)} %get-tuple-element.19, bf16[256,16,576]{2,0,1:T(8,128)(2,1)} %all-gather.3.cloned.1.call-done, bf16[1024,576]{0,1:T(8,128)(2,1)} %all-gather.5.cloned.1.call-done), kind=kOutput, calls=%fused_computation.2 | convolution fusion | flops 2422206464 | bytes 14238208 | tf_op jit(solution)/shard_map/qhd,kd->qhk/dot_general | solution.py:65
  135.1 0.0 copy-done.3
  135.1 0.0 copy-done.5
  135.1 0.0 copy-start.4
  135.1 5.9 %select_reduce_fusion.1 = (f32[256,16]{0,1:T(8,128)S(1)}, f32[256,16,512]{2,0,1:T(8,128)}) fusion(pred[512]{0:T(512)(128)(4,1)S(1)} %get-tuple-element.20, bf16[256,16,576]{2,0,1:T(8,128)(2,1)S(1)} %copy-done.3, bf16[1024,576]{0,1:T(8,128)(2,1)S(1)} %copy-done.5), kind=kOutput, calls=%fused_computation.4 | convolution fusion | flops 2422206464 | bytes 14238208 | tf_op jit(solution)/shard_map/qhd,kd->qhk/dot_general | solution.py:65
  141.0 0.0 copy-done.4
  141.0 1.5 select_reduce_fusion.2
  142.5 112.1 %pmax.7 = f32[256,16]{0,1:T(8,128)S(1)} all-reduce(f32[256,16]{0,1:T(8,128)S(1)} %get-tuple-element.9), channel_id=1, replica_groups=mesh['ctx'=32,'head'=8] {'ctx'}, use_global_device_ids=true, to_apply=%region_3.4 | all-reduce | flops 4096 | bytes 32768 | tf_op jit(solution)/shard_map/pmax | solution.py:79
  254.5 0.0 copy-start.1
  254.5 0.1 fusion.21
  254.6 0.0 copy-start.2
  254.6 4.7 fusion
  259.3 1.1 copy-done.1
  260.4 2.2 fusion.2
  262.6 0.1 copy-done.2
  262.8 2.5 fusion.6
  265.3 2.5 fusion.4
  267.8 5.1 add_multiply_fusion
  272.9 0.0 copy-start.6
  272.9 0.0 reduce-scatter.3.cloned.1.call-update
  272.9 0.6 copy-done.6
  273.6 0.6 dynamic-slice
  274.8 110.2 %all-reduce = f32[256,16]{0,1:T(8,128)S(1)} all-reduce(f32[256,16]{0,1:T(8,128)S(1)} %get-tuple-element.5), channel_id=3, replica_groups=mesh['ctx'=32,'head'=8] {'ctx'}, use_global_device_ids=true, to_apply=%region_8.9.clone | all-reduce | flops 4096 | bytes 32768
  385.0 0.1 constant_dynamic-slice_fusion
  385.1 140.2 %reduce-scatter.3.cloned.1.call-done = f32[8,16,512]{2,0,1:T(8,128)} async-done(((f32[256,16,512]{2,0,1:T(8,128)}), f32[8,16,512]{2,0,1:T(8,128)}) %reduce-scatter.3.cloned.1.call-update) | async-done | bytes 262160 | tf_op jit(solution)/shard_map/reduce_scatter | solution.py:82
  525.3 2.6 fusion.18
  527.9 0.6 copy.12
  (6 shorter events, 0.1 us)
Async XLA Ops:
  6.5 2.3 copy-start
  6.5 33.2 %all-gather.5.cloned.1.call-start = ((), (), s32[]{:S(2)}) async-start(), calls=%async_computation.2 | async-start | bytes 1327104 | tf_op jit(solution)/shard_map/all_gather | solution.py:46
  7.3 118.3 %all-gather.3.cloned.1.call-start = ((), (), s32[]{:S(2)}) async-start(), calls=%async_computation.1 | async-start | bytes 5406720 | tf_op jit(solution)/shard_map/all_gather | solution.py:53
  9.9 515.4 %reduce-scatter.3.cloned.1.call-start = ((), (), s32[]{:S(2)}) async-start(), calls=%async_computation.3 | async-start | bytes 8650752 | tf_op jit(solution)/shard_map/reduce_scatter | solution.py:82
  125.5 9.6 %copy-start.3 = (bf16[256,16,576]{2,0,1:T(8,128)(2,1)S(1)}, bf16[256,16,576]{2,0,1:T(8,128)(2,1)}, u32[]{:S(2)}) copy-start(bf16[256,16,576]{2,0,1:T(8,128)(2,1)} %all-gather.3.cloned.1.call-done) | copy-start | bytes 14155780
  125.5 9.6 %copy-start.5 = (bf16[1024,576]{0,1:T(8,128)(2,1)S(1)}, bf16[1024,576]{0,1:T(8,128)(2,1)}, u32[]{:S(2)}) copy-start(bf16[1024,576]{0,1:T(8,128)(2,1)} %all-gather.5.cloned.1.call-done) | copy-start | bytes 3538948
  135.1 5.9 %copy-start.4 = (bf16[8,576]{1,0:T(8,128)(2,1)S(1)}, bf16[8,576]{1,0:T(8,128)(2,1)}, u32[]{:S(2)}) copy-start(bf16[8,576]{1,0:T(8,128)(2,1)} %param.10) | copy-start | bytes 27652
  254.5 5.8 %copy-start.1 = (f32[256,16,512]{2,0,1:T(8,128)S(1)}, f32[256,16,512]{2,0,1:T(8,128)}, u32[]{:S(2)}) copy-start(f32[256,16,512]{2,0,1:T(8,128)} %get-tuple-element.16) | copy-start | bytes 25165828
  254.6 8.2 %copy-start.2 = (f32[256,16,512]{2,0,1:T(8,128)S(1)}, f32[256,16,512]{2,0,1:T(8,128)}, u32[]{:S(2)}) copy-start(f32[256,16,512]{2,0,1:T(8,128)} %get-tuple-element.18) | copy-start | bytes 25165828
  272.9 0.7 copy-start.6
Sparse Core Ops, SparseCore 0:
  9.2 30.5 all-gather.4
  42.4 83.0 all-gather.2
  273.1 252.2 reduce-scatter.2
where the time goes:
time: 538 us; the launch traced here: 535 us
  waiting for transfers between devices  256 us (48%)
  blocking collectives  222 us (41%)
  matrix products  30 us (6%)
  between operations  14.5 us (3%)
  other arithmetic  7.78 us (1%)
    reduce_scatter x1, waiting for transfers between devices, body(): lax.psum_scatter(run_acc * factor[:, :, None], 'ctx', scatter_dimension=0...  140 us
    pmax x1, blocking collectives, body(): best_top = lax.pmax(run_top, 'ctx')  112 us
    unnamed x1, blocking collectives  110 us
    all_gather x1, waiting for transfers between devices, body(): q_piece = lax.all_gather(absorbed, 'ctx', axis=0, tiled=True)  85.8 us
    all_gather x1, waiting for transfers between devices, body(): local_keys = lax.all_gather(cache, 'head', axis=0, tiled=True)  29 us
    dot_general x2, matrix products, body(): jnp.einsum('qhd,kd->qhk', q_piece, key_block, preferred_element_type=jnp....  15.4 us
  transfers between devices with their start and end apart: 3, of which 3 were waited for; matrix products, arithmetic and copies ran while one was open for 1% of the time, Pallas kernels for 0%

commit v1 on v0

v1 whole, which is shorter than its diff:
```python
import math

import jax
import jax.numpy as jnp
from jax import lax
from jax.experimental import pallas as pl
from jax.experimental.pallas import tpu as pltpu
from jax.sharding import PartitionSpec as P

f32 = jnp.float32
bf16 = jnp.bfloat16
NEG = -1e30
LOG2E = 1.4426950408889634
MESH = pl.DeviceIdType.MESH

NZ, NX, NY = 8, 4, 4
BLK = 128
WIDE = 640
LAT = 512
NEW_ROWS = 64
CH = 4 * BLK
FIRST = NEW_ROWS + CH
ROWS = 1024

ORDER = [
    (0, 0, 0), (1, 0, 0), (0, 1, 0), (0, 2, 0),
    (0, 0, 1), (0, 0, 2), (1, 1, 0), (1, 2, 0),
    (1, 0, 1), (1, 0, 2), (0, 3, 0), (0, 0, 3),
    (0, 1, 1), (0, 1, 2), (0, 2, 1), (0, 2, 2),
    (1, 3, 0), (1, 0, 3), (1, 1, 1), (1, 1, 2),
    (1, 2, 1), (1, 2, 2), (0, 3, 1), (0, 3, 2),
    (0, 1, 3), (0, 2, 3), (1, 3, 1), (1, 3, 2),
    (1, 1, 3), (1, 2, 3), (0, 3, 3), (1, 3, 3),
]
PLACE = {b: NEW_ROWS + BLK * n for n, b in enumerate(ORDER)}


def dot_t(a, b):
    return lax.dot_general(a, b, (((1,), (1,)), ((), ())), preferred_element_type=f32)


def dot_n(a, b):
    return jnp.dot(a, b, preferred_element_type=f32)


def kernel(
    scale, q_ref, cache_ref, new_ref, len_ref, wk_hbm, wv_hbm, out_ref,
    kbuf, nsend, qsend, qrecv, qabs, qn, wk, wv, sa, sb, pa, pb, al, top, tot, acc, ob, osend, orecv, ssend, srecv,
    w_sem, send_sem, k_sem, s_sem, q_sem, n_sem, o_sem, t_sem,
):
    ctx = lax.axis_index("ctx")
    head = lax.axis_index("head")
    z, x = ctx // NX, ctx % NX
    y, c = head // 2, head % 2

    def at(zz, xx, yy, cc):
        return (zz * NX + xx, yy * 2 + cc)

    step1x, step1y = 1 - c, c
    ax1p = at(z, (x + step1x) % NX, (y + step1y) % NY, c)
    ax1m = at(z, (x + 3 * step1x) % NX, (y + 3 * step1y) % NY, c)
    ax2p = at(z, (x + step1y) % NX, (y + step1x) % NY, c)
    ax2m = at(z, (x + 3 * step1y) % NX, (y + 3 * step1x) % NY, c)
    sib = at(z, x, y, 1 - c)
    z_to = [None] + [at((z + d) % NZ, x, y, c) for d in range(1, NZ)]
    z_back = [None] + [at((z + NZ - d) % NZ, x, y, c) for d in range(1, NZ)]
    x_to = [None] + [at(z, (x + d) % NX, y, c) for d in range(1, NX)]

    wk_copy = pltpu.make_async_copy(wk_hbm, wk, w_sem.at[0])
    wv_copy = pltpu.make_async_copy(wv_hbm, wv, w_sem.at[1])
    wk_copy.start()
    wv_copy.start()

    barrier = pltpu.get_barrier_semaphore()
    partners = [ax1p, ax1m, ax2p, ax2m, sib] + z_to[1:] + x_to[1:]
    for who in partners:
        pl.semaphore_signal(barrier, inc=1, device_id=who, device_id_type=MESH)

    length = len_ref[0]
    own = PLACE[(0, 0, 0)]
    slot = ctx * (NY * 2 * BLK) + head * BLK + lax.broadcasted_iota(jnp.int32, (BLK, 64), 0)
    bias = jnp.where(slot < length, 0.0, NEG).astype(bf16)
    kbuf[own : own + BLK, 0:LAT] = cache_ref[:, 0:LAT]
    kbuf[own : own + BLK, LAT:WIDE] = jnp.concatenate([cache_ref[:, LAT:576], bias], axis=1)
    qsend[0:128, :] = q_ref[:, 0:128]
    qsend[128:192, :] = jnp.concatenate([q_ref[0:64, 128:192], q_ref[64:128, 128:192]], axis=1)
    fresh = new_ref[...].astype(f32)
    fresh = jnp.concatenate([fresh, jnp.zeros((8, 576), f32)], axis=0)
    fresh = jnp.concatenate([fresh, jnp.zeros((16, 64), f32)], axis=1).astype(bf16)
    kbuf[0:16, :] = fresh
    nsend[...] = fresh

    pl.semaphore_wait(barrier, len(partners))

    sent = {}

    def send(key, src, dst, who, recv):
        number = sent[key][0] if key in sent else len(sent)
        copy = pltpu.make_async_remote_copy(
            src_ref=src, dst_ref=dst, send_sem=send_sem.at[number], recv_sem=recv, device_id=who, device_id_type=MESH
        )
        sent[key] = (number, src)
        copy.start()

    def rows_of(block, half=None):
        lo = PLACE[block]
        if half is None:
            return kbuf.at[lo : lo + BLK]
        return kbuf.at[lo + 64 * half : lo + 64 * half + 64]

    def k_send(block, to_block, who, half=None):
        _, d1, d2 = to_block
        key = ("k", to_block, half)
        send(key, rows_of(block, half), rows_of(to_block, half), who, k_sem.at[d1 * 4 + d2, half or 0])

    def sib_send(d1, d2):
        send(("s", d1, d2), rows_of((0, d1, d2)), rows_of((1, d1, d2)), sib, s_sem.at[d1 * 4 + d2])

    def wait_at(ref, sem):
        pltpu.make_async_copy(ref, ref, sem).wait()

    def wait_sib(d1, d2):
        wait_at(rows_of((1, d1, d2)), s_sem.at[d1 * 4 + d2])

    def event(d1, d2):
        block = (0, d1, d2)
        sem = d1 * 4 + d2
        if d2 == 3 or (d1, d2) == (3, 0):
            wait_at(rows_of(block, 0), k_sem.at[sem, 0])
            wait_at(rows_of(block, 1), k_sem.at[sem, 1])
        else:
            wait_at(rows_of(block), k_sem.at[sem, 0])
        if d2 == 0:
            if d1 == 1:
                k_send(block, (0, 3, 0), ax1p, 0)
            if d1 == 2:
                k_send(block, (0, 3, 0), ax1m, 1)
            k_send(block, (0, d1, 1), ax2p)
            k_send(block, (0, d1, 2), ax2m)
        elif d2 == 1:
            k_send(block, (0, d1, 3), ax2p, 0)
        elif d2 == 2:
            k_send(block, (0, d1, 3), ax2m, 1)
        sib_send(d1, d2)

    for d in (1, 7, 2, 6, 3, 5, 4):
        send(("q", d), qsend, qrecv.at[d], z_to[d], q_sem.at[d])
    mine = (0, 0, 0)
    k_send(mine, (0, 1, 0), ax1p)
    k_send(mine, (0, 2, 0), ax1m)
    k_send(mine, (0, 0, 1), ax2p)
    k_send(mine, (0, 0, 2), ax2m)
    sib_send(0, 0)
    for d in range(1, NX):
        send(("n", d), nsend, kbuf.at[16 * d : 16 * d + 16], x_to[d], n_sem.at[d])

    event(1, 0)
    event(2, 0)
    event(0, 1)
    event(0, 2)

    lane64 = lax.broadcasted_iota(jnp.int32, (128, 64), 1)
    row_j = lax.broadcasted_iota(jnp.int32, (128, 64), 0) // 16
    for d in range(NZ):
        if d:
            wait_at(qrecv.at[d], q_sem.at[d])
        block = qsend if d == 0 else qrecv.at[d]
        at_d = slice(128 * d, 128 * d + 128)
        qn[at_d, :] = block[0:128, :].astype(f32)
        rope = block[128:192, :]
        rope = jnp.concatenate([rope[:, 0:64], rope[:, 64:128]], axis=0)
        pick = jnp.where(lane64 == d * 8 + row_j, 1.0, 0.0).astype(bf16)
        qabs[at_d, LAT:WIDE] = jnp.concatenate([rope, pick], axis=1)
    event(3, 0)
    wk_copy.wait()
    for h in range(16):
        part = qn[pl.ds(h, 64, stride=16), :].astype(bf16)
        lat = dot_n(part, wk[h])
        for n in range(4):
            acc[n, pl.ds(h, 64, stride=16), :] = lat[:, 128 * n : 128 * n + 128]
    for t in range(16):
        r = slice(64 * t, 64 * t + 64)
        for n in range(4):
            qabs[r, 128 * n : 128 * n + 128] = acc[n, r, :].astype(bf16)

    for d in range(1, NX):
        wait_at(kbuf.at[16 * d : 16 * d + 16], n_sem.at[d])
    tail = kbuf[0:NEW_ROWS, LAT:WIDE].astype(f32)
    n_row = lax.broadcasted_iota(jnp.int32, (NEW_ROWS, 128), 0)
    col = lax.broadcasted_iota(jnp.int32, (NEW_ROWS, 128), 1) - 64
    n_j = n_row % 16
    n_rank = n_j * (NZ * NX) + z * NX + (x + NX - n_row // 16) % NX
    q_rank = (col % 8) * (NZ * NX) + (z + NZ - col // 8) % NZ * NX + x
    n_bias = jnp.where((n_j < 8) & (n_rank <= q_rank), 0.0, NEG)
    kbuf[0:NEW_ROWS, LAT:WIDE] = jnp.where(col >= 0, n_bias, tail).astype(bf16)

    event(1, 1)
    event(1, 2)
    event(2, 1)
    event(2, 2)
    event(0, 3)

    def scores(base, size, s):
        for lo in range(0, size, 256):
            n = min(256, size - lo)
            k = kbuf[pl.ds(base + lo, n), :]
            s[:, lo : lo + n] = dot_t(qabs[...], k)

    def weigh(size, s, p, first):
        for t in range(ROWS // 32):
            r = slice(32 * t, 32 * t + 32)
            sc = s[r, 0:size]
            new_top = jnp.broadcast_to(jnp.max(sc, axis=1, keepdims=True), (32, 128))
            if not first:
                old_top = top[r, :]
                new_top = jnp.maximum(old_top, new_top)
                shrink = jnp.exp2((old_top - new_top) * scale)
                al[r, :] = shrink
            top[r, :] = new_top
            w = jnp.exp2((sc - new_top[:, 0:1]) * scale)
            part = w[:, 0:128]
            for lo in range(128, CH, 128):
                part = part + w[:, lo : lo + 128]
            if size > CH:
                part = part + jnp.concatenate([w[:, CH:size], jnp.zeros((32, 128 - (size - CH)), f32)], axis=1)
            if not first:
                part = part + tot[r, :] * shrink
            tot[r, :] = part
            p[r, 0:size] = w.astype(bf16)

    def mix(base, size, p, first):
        for n in range(2):
            v = kbuf[pl.ds(base, size), 256 * n : 256 * n + 256]
            for t in range(ROWS // 256):
                r = slice(256 * t, 256 * t + 256)
                o = dot_n(p[r, 0:size], v)
                for k in range(2):
                    part = o[:, 128 * k : 128 * k + 128]
                    m = 2 * n + k
                    acc[m, r, :] = part if first else acc[m, r, :] * al[r, :] + part

    def base_of(step):
        return pl.multiple_of(NEW_ROWS + step * CH, 64)

    wait_sib(0, 0)
    scores(0, FIRST, sa)
    for d in ((1, 0), (2, 0)):
        wait_sib(*d)
    scores(base_of(1), CH, sb)
    weigh(FIRST, sa, pa, True)
    mix(0, FIRST, pa, True)
    event(3, 1)
    event(3, 2)

    def arrive(step):
        if step == 1:
            wait_sib(0, 1)
            wait_sib(0, 2)
        elif step == 2:
            event(1, 3)
            event(2, 3)
        elif step == 3:
            event(3, 3)
            for d in ((3, 0), (0, 3), (1, 1), (1, 2)):
                wait_sib(*d)
        elif step == 4:
            wait_sib(2, 1)
            wait_sib(2, 2)
        elif step == 5:
            wait_sib(3, 1)
            wait_sib(3, 2)
        else:
            wait_sib(1, 3)
            wait_sib(2, 3)
            wait_sib(3, 3)

    def pair(g, carry):
        for k in range(2):
            for gg in range(3):
                pl.when(g == gg)(lambda step=1 + 2 * gg + k: arrive(step))
            step = 1 + 2 * g + k
            s_now, s_next, p = (sb, sa, pb) if k == 0 else (sa, sb, pa)
            scores(base_of(step + 1), CH, s_next)
            weigh(CH, s_now, p, False)
            mix(base_of(step), CH, p, False)
        return carry

    lax.fori_loop(0, 3, pair, 0)
    weigh(CH, sb, pb, False)
    mix(base_of(7), CH, pb, False)

    lane = lax.broadcasted_iota(jnp.int32, (128, 128), 1)
    for d in range(NZ):
        r = slice(128 * d, 128 * d + 128)
        total = jnp.sum(tot[r, :], axis=1, keepdims=True)
        ssend[d] = jnp.where(lane == 0, top[r, :], total).T[0:8, :]
        if d:
            send(("t", d), ssend.at[d], srecv.at[d], z_back[d], t_sem.at[d])
    wv_copy.wait()
    for h in range(16):
        part = jnp.concatenate([acc[n, pl.ds(h, 64, stride=16), :] for n in range(4)], axis=1)
        hi = part.astype(bf16)
        lo = (part - hi.astype(f32)).astype(bf16)
        both = dot_n(jnp.concatenate([hi, lo], axis=0), wv[h])
        ob[pl.ds(h, 64, stride=16), :] = both[0:64] + both[64:128]
    for d in range(1, NZ):
        osend[d] = ob[128 * d : 128 * d + 128, :].astype(bf16)
        send(("o", d), osend.at[d], orecv.at[d], z_back[d], o_sem.at[d])

    for d in range(1, NZ):
        wait_at(srecv.at[d], t_sem.at[d])
    tops = [ssend[0, 0:1, :]] + [srecv[d, 0:1, :] for d in range(1, NZ)]
    totals = [ssend[0, 1:2, :]] + [srecv[d, 1:2, :] for d in range(1, NZ)]
    best = tops[0]
    for d in range(1, NZ):
        best = jnp.maximum(best, tops[d])
    shares = [jnp.exp2((t - best) * scale) for t in tops]
    full = shares[0] * totals[0]
    for d in range(1, NZ):
        full = full + shares[d] * totals[d]
    shares = [s / full for s in shares]
    by_row = jnp.concatenate(shares + [jnp.zeros((120, 128), f32)], axis=0).T
    result = ob[0:128, :] * by_row[:, 0:1]
    for d in range(1, NZ):
        wait_at(orecv.at[d], o_sem.at[d])
        result = result + orecv[d].astype(f32) * by_row[:, d : d + 1]
    out_ref[...] = result.astype(bf16)
    for number, src in sent.values():
        pltpu.make_async_copy(src, src, send_sem.at[number]).wait()


def body(queries, absorb_k, absorb_v, cache, new_entries, cache_len):
    scale = LOG2E / math.sqrt(queries.shape[2])
    vmem = pl.BlockSpec(memory_space=pltpu.VMEM)
    hbm = pl.BlockSpec(memory_space=pl.ANY)
    dma = pltpu.SemaphoreType.DMA

    def run(*refs):
        kernel(scale, *refs)

    out = pl.pallas_call(
        run,
        out_shape=jax.ShapeDtypeStruct((128, 128), bf16),
        in_specs=[vmem, vmem, vmem, pl.BlockSpec(memory_space=pltpu.SMEM), hbm, hbm],
        out_specs=vmem,
        scratch_shapes=[
            pltpu.VMEM((NEW_ROWS + 32 * BLK, WIDE), bf16),
            pltpu.VMEM((16, WIDE), bf16),
            pltpu.VMEM((192, 128), bf16),
            pltpu.VMEM((NZ, 192, 128), bf16),
            pltpu.VMEM((ROWS, WIDE), bf16),
            pltpu.VMEM((ROWS, 128), f32),
            pltpu.VMEM((16, 128, LAT), bf16),
            pltpu.VMEM((16, LAT, 128), bf16),
            pltpu.VMEM((ROWS, WIDE), f32),
            pltpu.VMEM((ROWS, CH), f32),
            pltpu.VMEM((ROWS, WIDE), bf16),
            pltpu.VMEM((ROWS, CH), bf16),
            pltpu.VMEM((ROWS, 128), f32),
            pltpu.VMEM((ROWS, 128), f32),
            pltpu.VMEM((ROWS, 128), f32),
            pltpu.VMEM((4, ROWS, 128), f32),
            pltpu.VMEM((ROWS, 128), f32),
            pltpu.VMEM((NZ, 128, 128), bf16),
            pltpu.VMEM((NZ, 128, 128), bf16),
            pltpu.VMEM((NZ, 8, 128), f32),
            pltpu.VMEM((NZ, 8, 128), f32),
            dma((2,)),
            dma((80,)),
            dma((16, 2)),
            dma((16,)),
            dma((NZ,)),
            dma((NX,)),
            dma((NZ,)),
            dma((NZ,)),
        ],
        compiler_params=pltpu.CompilerParams(
            collective_id=0, has_side_effects=True, vmem_limit_bytes=56 << 20
        ),
    )(queries.reshape(128, 192), cache, new_entries, cache_len, absorb_k, absorb_v)
    return out.reshape(8, 16, 128)


def solution(mesh):
    in_specs = (
        P("ctx", "head", None),
        P("head", None, None),
        P("head", None, None),
        P(("ctx", "head"), None),
        P("ctx", None),
        P(),
    )
    out_specs = P("ctx", "head", None)
    return jax.shard_map(body, mesh=mesh, in_specs=in_specs, out_specs=out_specs, check_vma=False)
```

time: 538 us -> 53.9 us (0.10)
  waiting for transfers between devices: 256 us -> 0 us
  blocking collectives: 222 us -> 0 us
  Pallas kernels: 0 us -> 49.8 us
  matrix products: 30 us -> 0 us
  between operations: 14.5 us -> 0.66 us
  other arithmetic: 7.78 us -> 0 us
    reduce_scatter x1 -> x0, waiting for transfers between devices: 140 us -> none  [body(): lax.psum_scatter(run_acc * factor[:, :, None], 'ctx', scatter_dimension=0...]
    all_gather x2 -> x0, waiting for transfers between devices: 115 us -> none  [the longest x1 85.8 us: body(): q_piece = lax.all_gather(absorbed, 'ctx', axis=0, tiled=True)]
    pmax x1 -> x0, blocking collectives: 112 us -> none  [body(): best_top = lax.pmax(run_top, 'ctx')]
    unnamed x1 -> x0, blocking collectives: 110 us -> none
    pallas_call x0 -> x1, Pallas kernels: none -> 49.8 us  [body(): pl.pallas_call(run, out_shape=jax.ShapeDtypeStruct((128, 128), bf16), in_...]
    dot_general x8 -> x0, matrix products: 30 us -> none  [the longest x2 15.4 us: body(): jnp.einsum('qhd,kd->qhk', q_piece, key_block, preferred_element_type=jnp....]
    reduce_sum x3 -> x0, other arithmetic: 6.96 us -> none  [online_update(): run_total = run_total * rescale + jnp.sum(weights, axis=2)]
  transfers between devices with their start and end apart: 3 -> 0, of which waited for: 3 -> 0; matrix products, arithmetic and copies ran while one was open for 1% -> 0% of each run, Pallas kernels for 0% -> 0%
where the time goes in v1:
time: 53.9 us; the launch traced here: 53.5 us
  Pallas kernels  49.8 us (92%)
  local copies, waits for them, and re-layouts  3.07 us (6%)
  between operations  0.66 us (1%)
    pallas_call x1, Pallas kernels, body(): pl.pallas_call(run, out_shape=jax.ShapeDtypeStruct((128, 128), bf16), in_...  49.8 us
    unnamed x2, local copies, waits for them, and re-layouts  3.07 us

profile of v1, /device:TPU:1, one launch (start us, length us, event | category | flops | bytes accessed | tf_op | source)
XLA Modules:
  0.0 53.5 jit_solution(13617905495367762860)
XLA Ops:
  0.7 1.7 %copy.7.refs_1_ = bf16[128,576]{1,0:T(8,128)(2,1)} copy(bf16[128,576]{0,1:T(8,128)(2,1)} %param.9) | data formatting | bytes 294912 | tf_op args[3]
  2.4 49.8 %shard_map.64 = bf16[128,128]{1,0:T(8,128)(2,1)} custom-call(bf16[128,192]{1,0:T(8,128)(2,1)} %bitcast.3, bf16[128,576]{1,0:T(8,128)(2,1)} %copy.7.refs_1_, bf16[8,576]{1,0:T(8,128)(2,1)} %refs_2_.1, s32[1]{0:T(128)S(6)} %copy.9.refs_3_, bf16[16,128,512]{2,1,0:T(8,128)(2,1)} %refs_4_.1, bf16[16,512,128]{2,1,0:T(8,128)(2,1)} %refs_5_.1), custom_call_target="tpu_custom_call" | custom-call | tf_op jit(solution)/shard_map/pallas_call | solution.py:341
  52.1 1.4 %copy.10 = bf16[8,16,128]{2,1,0:T(8,128)(2,1)} copy(bf16[8,16,128]{2,1,0:T(8,128)(2,1)} %bitcast.2) | data formatting | bytes 65536

commit v2 on v1

v2 whole, which is shorter than its diff:
```python
import math

import jax
import jax.numpy as jnp
from jax import lax
from jax.experimental import pallas as pl
from jax.experimental.pallas import tpu as pltpu
from jax.sharding import PartitionSpec as P

f32 = jnp.float32
bf16 = jnp.bfloat16
NEG = -1e30
LOG2E = 1.4426950408889634
MESH = pl.DeviceIdType.MESH

NZ, NX, NY = 8, 4, 4
BLK = 128
PACK = 144
LAT = 512
NEW_ROWS = 64
CH = 4 * BLK
HALF = 512
ROWS = 2 * HALF

NEAR = (0, 1, 7, 2)
FAR = (6, 3, 5, 4)
SPOT = {d: n for n, d in enumerate(NEAR + FAR)}

ORDER = [
    (0, 0, 0), (1, 0, 0), (0, 1, 0), (0, 2, 0),
    (0, 0, 1), (0, 0, 2), (1, 1, 0), (1, 2, 0),
    (1, 0, 1), (1, 0, 2), (0, 3, 0), (0, 0, 3),
    (0, 1, 1), (0, 1, 2), (0, 2, 1), (0, 2, 2),
    (1, 3, 0), (1, 0, 3), (1, 1, 1), (1, 1, 2),
    (1, 2, 1), (1, 2, 2), (0, 3, 1), (0, 3, 2),
    (0, 1, 3), (0, 2, 3), (1, 3, 1), (1, 3, 2),
    (1, 1, 3), (1, 2, 3), (0, 3, 3), (1, 3, 3),
]
PLACE = {b: n for n, b in enumerate(ORDER)}
OFFSET = (0, 3, 1, 2)

N, F = 0, 1
UNITS = [
    (N, 0), (N, 1), (F, 0), (F, 1), (N, 2), (F, 2), (N, 3), (F, 3),
    (N, 4), (F, 4), (N, 5), (F, 5), (F, 6), (F, 7), (N, 6), (N, 7),
]
PASS = {
    0: [(1, 0), (2, 0), (0, 1), (0, 2)],
    4: [(3, 0), (0, 3), (1, 1), (1, 2), (2, 1), (2, 2)],
    8: [(3, 1), (3, 2)],
    10: [(1, 3), (2, 3)],
    12: [(3, 3)],
}


def dot_t(a, b):
    return lax.dot_general(a, b, (((1,), (1,)), ((), ())), preferred_element_type=f32)


def dot_n(a, b):
    return jnp.dot(a, b, preferred_element_type=f32)


def kernel(
    scale, q_ref, cache_ref, new_ref, len_ref, wk_hbm, wv_hbm, out_ref,
    kbuf, ktail, nsend, nbuf, qsend, qrecv, qabs, qn, wk, wv, sa, sb, pa, pb, al, top, tot, acc, ob, osend, orecv, ssend, srecv,
    w_sem, send_sem, k_sem, s_sem, q_sem, n_sem, o_sem, t_sem,
):
    ctx = lax.axis_index("ctx")
    head = lax.axis_index("head")
    z, x = ctx // NX, ctx % NX
    y, c = head // 2, head % 2

    def at(zz, xx, yy, cc):
        return (zz * NX + xx, yy * 2 + cc)

    on_x, on_y = 1 - c, c
    ax1p = at(z, (x + on_x) % NX, (y + on_y) % NY, c)
    ax1m = at(z, (x + 3 * on_x) % NX, (y + 3 * on_y) % NY, c)
    ax2p = at(z, (x + on_y) % NX, (y + on_x) % NY, c)
    ax2m = at(z, (x + 3 * on_y) % NX, (y + 3 * on_x) % NY, c)
    sib = at(z, x, y, 1 - c)
    z_to = [None] + [at((z + d) % NZ, x, y, c) for d in range(1, NZ)]
    x_to = [None] + [at(z, (x + d) % NX, y, c) for d in range(1, NX)]

    wk_copy = pltpu.make_async_copy(wk_hbm, wk, w_sem.at[0])
    wv_copy = pltpu.make_async_copy(wv_hbm, wv, w_sem.at[1])
    wk_copy.start()
    wv_copy.start()

    barrier = pltpu.get_barrier_semaphore()
    partners = [ax1p, ax1m, ax2p, ax2m, sib] + z_to[1:] + x_to[1:]
    for who in partners:
        pl.semaphore_signal(barrier, inc=1, device_id=who, device_id_type=MESH)

    length = len_ref[0]
    mine = kbuf.at[0]
    qsend[0:128, :] = q_ref[:, 0:128]
    qsend[128:192, :] = jnp.concatenate([q_ref[0:64, 128:192], q_ref[64:128, 128:192]], axis=1)
    for n in range(4):
        mine[0:128, 128 * n : 128 * n + 128] = cache_ref[128 * n : 128 * n + 128, :].astype(f32).T.astype(bf16)
    rope = jnp.concatenate([cache_ref[LAT:576, :].astype(f32), jnp.zeros((64, 128), f32)], axis=0).T
    mine[128:144, :] = jnp.concatenate([rope[16 * g : 16 * g + 16, 0:64] for g in range(8)], axis=1).astype(bf16)
    fresh = new_ref[...].astype(f32)
    fresh = jnp.concatenate([fresh, jnp.zeros((8, 576), f32)], axis=0)
    fresh = jnp.concatenate([fresh, jnp.zeros((16, 64), f32)], axis=1).astype(bf16)
    nbuf[0] = fresh
    nsend[...] = fresh

    pl.semaphore_wait(barrier, len(partners))

    sent = {}

    def send(key, src, dst, who, recv):
        number = len(sent)
        copy = pltpu.make_async_remote_copy(
            src_ref=src, dst_ref=dst, send_sem=send_sem.at[number], recv_sem=recv, device_id=who, device_id_type=MESH
        )
        sent[key] = (number, src)
        copy.start()

    def rows_of(block, half=None):
        ref = kbuf.at[PLACE[block]]
        return ref if half is None else ref.at[0:80] if half == 0 else ref.at[80:144]

    def k_send(block, to_block, who, half=None):
        _, d1, d2 = to_block
        key = ("k", to_block, half)
        send(key, rows_of(block, half), rows_of(to_block, half), who, k_sem.at[d1 * 4 + d2, half or 0])

    def sib_send(d1, d2):
        send(("s", d1, d2), rows_of((0, d1, d2)), rows_of((1, d1, d2)), sib, s_sem.at[d1 * 4 + d2])

    def wait_at(ref, sem):
        pltpu.make_async_copy(ref, ref, sem).wait()

    def wait_sib(d1, d2):
        wait_at(rows_of((1, d1, d2)), s_sem.at[d1 * 4 + d2])

    def event(d1, d2):
        block = (0, d1, d2)
        sem = d1 * 4 + d2
        if d2 == 3 or (d1, d2) == (3, 0):
            wait_at(rows_of(block, 0), k_sem.at[sem, 0])
            wait_at(rows_of(block, 1), k_sem.at[sem, 1])
        else:
            wait_at(rows_of(block), k_sem.at[sem, 0])
        if d2 == 0:
            if d1 == 1:
                k_send(block, (0, 3, 0), ax1p, 0)
            if d1 == 2:
                k_send(block, (0, 3, 0), ax1m, 1)
            k_send(block, (0, d1, 1), ax2p)
            k_send(block, (0, d1, 2), ax2m)
        elif d2 == 1:
            k_send(block, (0, d1, 3), ax2p, 0)
        elif d2 == 2:
            k_send(block, (0, d1, 3), ax2m, 1)
        sib_send(d1, d2)

    def q_send(d, to, half=None, src=None):
        part = slice(0, 192) if half is None else slice(96 * half, 96 * half + 96)
        src = qsend if src is None else src
        send(("q", d, half), src.at[part], qrecv.at[d, part], to, q_sem.at[d, half or 0])

    q_send(1, z_to[1])
    q_send(7, z_to[7])
    q_send(2, z_to[2])
    q_send(6, z_to[6])
    own = (0, 0, 0)
    k_send(own, (0, 1, 0), ax1p)
    k_send(own, (0, 2, 0), ax1m)
    k_send(own, (0, 0, 1), ax2p)
    k_send(own, (0, 0, 2), ax2m)
    sib_send(0, 0)
    for d in range(1, NX):
        send(("n", d), nsend, nbuf.at[d], x_to[d], n_sem.at[d])

    def place(d):
        r = slice(128 * SPOT[d], 128 * SPOT[d] + 128)
        lane64 = lax.broadcasted_iota(jnp.int32, (128, 64), 1)
        row_j = lax.broadcasted_iota(jnp.int32, (128, 64), 0) // 16
        block = qsend if d == 0 else qrecv.at[d]
        qn[r, :] = block[0:128, :].astype(f32)
        rope = block[128:192, :]
        rope = jnp.concatenate([rope[:, 0:64], rope[:, 64:128]], axis=0)
        pick = jnp.where(lane64 == d * 8 + row_j, 1.0, 0.0).astype(bf16)
        qabs[r, LAT:640] = jnp.concatenate([rope, pick], axis=1)

    def absorb(half):
        for h in range(16):
            part = qn[pl.ds(HALF * half + h, 32, stride=16), :].astype(bf16)
            lat = dot_n(part, wk[h])
            for n in range(4):
                acc[n, pl.ds(HALF * half + h, 32, stride=16), :] = lat[:, 128 * n : 128 * n + 128]
        for t in range(8):
            r = slice(HALF * half + 64 * t, HALF * half + 64 * t + 64)
            for n in range(4):
                qabs[r, 128 * n : 128 * n + 128] = acc[n, r, :].astype(bf16)

    def unpack(block):
        plane, d1, d2 = block
        first_x = on_x if plane == 0 else on_y
        s1, s2 = OFFSET[d1], OFFSET[d2]
        sx = (x + s1 * first_x + s2 * (1 - first_x)) % NX
        sy = (y + s1 * (1 - first_x) + s2 * first_x) % NY
        sc = c if plane == 0 else 1 - c
        slot = ((z * NX + sx) * NY + sy) * (2 * BLK) + sc * BLK
        here = PLACE[block]
        packed = kbuf[here, 128:144, :].astype(f32)
        row = lax.broadcasted_iota(jnp.int32, (16, 128), 0)
        lane = lax.broadcasted_iota(jnp.int32, (16, 128), 1)
        for g in range(8):
            piece = packed[:, 128 * (g // 2) : 128 * (g // 2) + 128]
            if g % 2:
                piece = pltpu.roll(piece, 64, 1)
            bias = jnp.where(slot + 16 * g + row < length, 0.0, NEG)
            ktail[BLK * here + 16 * g : BLK * here + 16 * g + 16, :] = jnp.where(lane < 64, piece, bias).astype(bf16)

    def mask_new():
        for d in range(1, NX):
            wait_at(nbuf.at[d], n_sem.at[d])
        n_j = lax.broadcasted_iota(jnp.int32, (16, 128), 0)
        col = lax.broadcasted_iota(jnp.int32, (16, 128), 1) - 64
        q_rank = (col % 8) * (NZ * NX) + (z + NZ - col // 8) % NZ * NX + x
        for d in range(NX):
            n_rank = n_j * (NZ * NX) + z * NX + (x + NX - d) % NX
            bias = jnp.where((n_j < 8) & (n_rank <= q_rank), 0.0, NEG)
            tail = nbuf[d, :, LAT:640].astype(f32)
            nbuf[d, :, LAT:640] = jnp.where(col >= 0, bias, tail).astype(bf16)

    def keys_of(chunk, lo):
        if lo == CH:
            return jnp.concatenate([nbuf[d] for d in range(NX)], axis=0)
        b = chunk * 4 + lo // BLK
        lat = jnp.concatenate([kbuf[b, 0:128, :], kbuf[b + 1, 0:128, :]], axis=0)
        return jnp.concatenate([lat, ktail[BLK * b : BLK * b + 256, :]], axis=1)

    def scores(unit, s):
        half, chunk = unit
        q = qabs.at[HALF * half : HALF * half + HALF]
        for lo in range(0, CH, 256):
            s[:, lo : lo + 256] = dot_t(q[...], keys_of(chunk, lo))
        if chunk == 0:
            s[:, CH : CH + NEW_ROWS] = dot_t(q[...], keys_of(chunk, CH))

    def weigh(unit, s, p):
        half, chunk = unit
        size = CH + NEW_ROWS if chunk == 0 else CH
        for t in range(HALF // 32):
            sr = slice(32 * t, 32 * t + 32)
            r = slice(HALF * half + 32 * t, HALF * half + 32 * t + 32)
            sc = s[sr, 0:size]
            new_top = jnp.broadcast_to(jnp.max(sc, axis=1, keepdims=True), (32, 128))
            if chunk:
                old_top = top[r, :]
                new_top = jnp.maximum(old_top, new_top)
                shrink = jnp.exp2((old_top - new_top) * scale)
                al[sr, :] = shrink
            top[r, :] = new_top
            w = jnp.exp2((sc - new_top[:, 0:1]) * scale)
            part = w[:, 0:128]
            for lo in range(128, CH, 128):
                part = part + w[:, lo : lo + 128]
            if size > CH:
                part = part + jnp.concatenate([w[:, CH:size], jnp.zeros((32, 128 - NEW_ROWS), f32)], axis=1)
            if chunk:
                part = part + tot[r, :] * shrink
            tot[r, :] = part
            p[sr, 0:size] = w.astype(bf16)

    def mix(unit, p):
        half, chunk = unit
        size = CH + NEW_ROWS if chunk == 0 else CH
        for n in range(2):
            cols = slice(256 * n, 256 * n + 256)
            v = [kbuf[chunk * 4 + b, 0:128, cols] for b in range(4)]
            if chunk == 0:
                v = v + [nbuf[d, :, cols] for d in range(NX)]
            v = jnp.concatenate(v, axis=0)
            for t in range(HALF // 256):
                sr = slice(256 * t, 256 * t + 256)
                r = slice(HALF * half + 256 * t, HALF * half + 256 * t + 256)
                o = dot_n(p[sr, 0:size], v)
                for k in range(2):
                    part = o[:, 128 * k : 128 * k + 128]
                    m = 2 * n + k
                    acc[m, r, :] = part if chunk == 0 else acc[m, r, :] * al[sr, :] + part

    def deliver(half):
        lane = lax.broadcasted_iota(jnp.int32, (128, 128), 1)
        owners = NEAR if half == N else FAR
        for d in owners:
            r = slice(128 * SPOT[d], 128 * SPOT[d] + 128)
            total = jnp.sum(tot[r, :], axis=1, keepdims=True)
            ssend[d] = jnp.where(lane == 0, top[r, :], total).T[0:8, :]
            if d:
                send(("t", d), ssend.at[d], srecv.at[d], z_to[NZ - d], t_sem.at[d])
        for h in range(16):
            rows = pl.ds(HALF * half + h, 32, stride=16)
            part = jnp.concatenate([acc[n, rows, :] for n in range(4)], axis=1)
            hi = part.astype(bf16)
            lo = (part - hi.astype(f32)).astype(bf16)
            both = dot_n(jnp.concatenate([hi, lo], axis=0), wv[h])
            ob[rows, :] = both[0:32] + both[32:64]
        for d in owners:
            if d:
                osend[d] = ob[128 * SPOT[d] : 128 * SPOT[d] + 128, :].astype(bf16)
                send(("o", d), osend.at[d], orecv.at[d], z_to[NZ - d], o_sem.at[d])

    def take_near():
        place(0)
        wait_at(qrecv.at[2], q_sem.at[2, 0])
        q_send(3, z_to[1], src=qrecv.at[2])
        q_send(4, z_to[2], half=0, src=qrecv.at[2])
        wait_at(qrecv.at[6], q_sem.at[6, 0])
        q_send(5, z_to[7], src=qrecv.at[6])
        q_send(4, z_to[6], half=1, src=qrecv.at[6])
        wait_at(qrecv.at[1], q_sem.at[1, 0])
        wait_at(qrecv.at[7], q_sem.at[7, 0])
        for d in NEAR[1:]:
            place(d)

    def take_far():
        wait_at(qrecv.at[3], q_sem.at[3, 0])
        wait_at(qrecv.at[5], q_sem.at[5, 0])
        wait_at(qrecv.at[4, 0:96], q_sem.at[4, 0])
        wait_at(qrecv.at[4, 96:192], q_sem.at[4, 1])
        for d in FAR:
            place(d)

    ready = set()
    sib_in = set()

    def before(n):
        half, chunk = UNITS[n]
        if n == 0:
            take_near()
            wk_copy.wait()
            absorb(N)
        for b in PASS.get(n, ()):
            event(*b)
        if (half, chunk) == (F, 0):
            take_far()
            absorb(F)
        if n == 0:
            mask_new()
        if chunk in ready:
            return
        ready.add(chunk)
        for b in ORDER[4 * chunk : 4 * chunk + 4]:
            if b[0] == 1:
                wait_sib(*b[1:])
            unpack(b)

    before(0)
    scores(UNITS[0], sa)
    for n, unit in enumerate(UNITS):
        s_now, s_next, p = (sa, sb, pa) if n % 2 == 0 else (sb, sa, pb)
        if n + 1 < len(UNITS):
            before(n + 1)
            scores(UNITS[n + 1], s_next)
        weigh(unit, s_now, p)
        mix(unit, p)
        if unit == (F, 7):
            wv_copy.wait()
            deliver(F)
    deliver(N)

    for d in range(1, NZ):
        wait_at(srecv.at[d], t_sem.at[d])
    tops = [ssend[0, 0:1, :]] + [srecv[d, 0:1, :] for d in range(1, NZ)]
    totals = [ssend[0, 1:2, :]] + [srecv[d, 1:2, :] for d in range(1, NZ)]
    best = tops[0]
    for d in range(1, NZ):
        best = jnp.maximum(best, tops[d])
    shares = [jnp.exp2((t - best) * scale) for t in tops]
    full = shares[0] * totals[0]
    for d in range(1, NZ):
        full = full + shares[d] * totals[d]
    shares = [s / full for s in shares]
    by_row = jnp.concatenate(shares + [jnp.zeros((120, 128), f32)], axis=0).T
    result = ob[0:128, :] * by_row[:, 0:1]
    for d in FAR + NEAR[1:]:
        wait_at(orecv.at[d], o_sem.at[d])
        result = result + orecv[d].astype(f32) * by_row[:, d : d + 1]
    out_ref[...] = result.astype(bf16)
    for number, src in sent.values():
        pltpu.make_async_copy(src, src, send_sem.at[number]).wait()


def body(queries, absorb_k, absorb_v, cache, new_entries, cache_len):
    scale = LOG2E / math.sqrt(queries.shape[2])
    vmem = pl.BlockSpec(memory_space=pltpu.VMEM)
    hbm = pl.BlockSpec(memory_space=pl.ANY)
    dma = pltpu.SemaphoreType.DMA

    def run(*refs):
        kernel(scale, *refs)

    out = pl.pallas_call(
        run,
        out_shape=jax.ShapeDtypeStruct((128, 128), bf16),
        in_specs=[vmem, vmem, vmem, pl.BlockSpec(memory_space=pltpu.SMEM), hbm, hbm],
        out_specs=vmem,
        scratch_shapes=[
            pltpu.VMEM((32, PACK, LAT), bf16),
            pltpu.VMEM((32 * BLK, 128), bf16),
            pltpu.VMEM((16, 640), bf16),
            pltpu.VMEM((NX, 16, 640), bf16),
            pltpu.VMEM((192, 128), bf16),
            pltpu.VMEM((NZ, 192, 128), bf16),
            pltpu.VMEM((ROWS, 640), bf16),
            pltpu.VMEM((ROWS, 128), f32),
            pltpu.VMEM((16, 128, LAT), bf16),
            pltpu.VMEM((16, LAT, 128), bf16),
            pltpu.VMEM((HALF, 640), f32),
            pltpu.VMEM((HALF, 640), f32),
            pltpu.VMEM((HALF, 640), bf16),
            pltpu.VMEM((HALF, 640), bf16),
            pltpu.VMEM((HALF, 128), f32),
            pltpu.VMEM((ROWS, 128), f32),
            pltpu.VMEM((ROWS, 128), f32),
            pltpu.VMEM((4, ROWS, 128), f32),
            pltpu.VMEM((ROWS, 128), f32),
            pltpu.VMEM((NZ, 128, 128), bf16),
            pltpu.VMEM((NZ, 128, 128), bf16),
            pltpu.VMEM((NZ, 8, 128), f32),
            pltpu.VMEM((NZ, 8, 128), f32),
            dma((2,)),
            dma((88,)),
            dma((16, 2)),
            dma((16,)),
            dma((NZ, 2)),
            dma((NX,)),
            dma((NZ,)),
            dma((NZ,)),
        ],
        compiler_params=pltpu.CompilerParams(
            collective_id=0, has_side_effects=True, vmem_limit_bytes=56 << 20
        ),
    )(queries.reshape(128, 192), cache.T, new_entries, cache_len, absorb_k, absorb_v)
    return out.reshape(8, 16, 128)


def solution(mesh):
    in_specs = (
        P("ctx", "head", None),
        P("head", None, None),
        P("head", None, None),
        P(("ctx", "head"), None),
        P("ctx", None),
        P(),
    )
    out_specs = P("ctx", "head", None)
    return jax.shard_map(body, mesh=mesh, in_specs=in_specs, out_specs=out_specs, check_vma=False)
```

time: 53.9 us -> 49.1 us (0.911)
  Pallas kernels: 49.8 us -> 46.9 us
  local copies, waits for them, and re-layouts: 3.07 us -> 1.38 us
    pallas_call x1, Pallas kernels: 49.8 us -> 46.9 us  [body(): pl.pallas_call(run, out_shape=jax.ShapeDtypeStruct((128, 128), bf16), in_...]
    unnamed x2 -> x1, local copies, waits for them, and re-layouts: 3.07 us -> 1.38 us
where the time goes in v2:
time: 49.1 us; the launch traced here: 48.9 us
  Pallas kernels  46.9 us (96%)
  local copies, waits for them, and re-layouts  1.38 us (3%)
  between operations  0.66 us (1%)
    pallas_call x1, Pallas kernels, body(): pl.pallas_call(run, out_shape=jax.ShapeDtypeStruct((128, 128), bf16), in_...  46.9 us
    unnamed x1, local copies, waits for them, and re-layouts  1.38 us

profile of v2, /device:TPU:1, one launch (start us, length us, event | category | flops | bytes accessed | tf_op | source)
XLA Modules:
  0.0 48.9 jit_solution(10417976221142193205)
XLA Ops:
  0.7 46.9 %shard_map.64 = bf16[128,128]{1,0:T(8,128)(2,1)} custom-call(bf16[128,192]{1,0:T(8,128)(2,1)} %bitcast.5, bf16[576,128]{1,0:T(8,128)(2,1)} %bitcast.3, bf16[8,576]{1,0:T(8,128)(2,1)} %refs_2_.1, s32[1]{0:T(128)S(6)} %copy.8.refs_3_, bf16[16,128,512]{2,1,0:T(8,128)(2,1)} %refs_4_.1, bf16[16,512,128]{2,1,0:T(8,128)(2,1)} %refs_5_.1), custom_call_target="tpu_custom_call" | custom-call | tf_op jit(solution)/shard_map/pallas_call | solution.py:401
  47.5 1.4 %copy.9 = bf16[8,16,128]{2,1,0:T(8,128)(2,1)} copy(bf16[8,16,128]{2,1,0:T(8,128)(2,1)} %bitcast.4) | data formatting | bytes 65536

commit v3 on v2

--- a/solution.py
+++ b/solution.py
@@ -41,15 +41,18 @@
 
 N, F = 0, 1
 UNITS = [
-    (N, 0), (N, 1), (F, 0), (F, 1), (N, 2), (F, 2), (N, 3), (F, 3),
-    (N, 4), (F, 4), (N, 5), (F, 5), (F, 6), (F, 7), (N, 6), (N, 7),
+    (N, 0), (N, 1), (F, 0), (F, 1), (N, 2), (F, 2), (F, 3), (F, 4),
+    (F, 5), (F, 6), (F, 7), (N, 3), (N, 4), (N, 5), (N, 6), (N, 7),
 ]
 PASS = {
     0: [(1, 0), (2, 0), (0, 1), (0, 2)],
-    4: [(3, 0), (0, 3), (1, 1), (1, 2), (2, 1), (2, 2)],
-    8: [(3, 1), (3, 2)],
-    10: [(1, 3), (2, 3)],
-    12: [(3, 3)],
+    2: [(3, 0), (0, 3)],
+    3: [(1, 1), (1, 2)],
+    4: [(2, 1), (2, 2)],
+    5: [(3, 1)],
+    6: [(3, 2), (1, 3)],
+    7: [(2, 3)],
+    8: [(3, 3)],
 }
 
 
@@ -62,8 +65,8 @@
 
 
 def kernel(
-    scale, q_ref, cache_ref, new_ref, len_ref, wk_hbm, wv_hbm, out_ref,
-    kbuf, ktail, nsend, nbuf, qsend, qrecv, qabs, qn, wk, wv, sa, sb, pa, pb, al, top, tot, acc, ob, osend, orecv, ssend, srecv,
+    scale, q_hbm, cache_hbm, new_hbm, len_ref, wk_hbm, wv_hbm, out_ref,
+    q_ref, cache_ref, new_ref, kbuf, ktail, nsend, nbuf, qsend, qrecv, qabs, qn, wk, wv, sa, sb, pa, pb, al, top, tot, acc, ob, osend, orecv, ssend, srecv,
     w_sem, send_sem, k_sem, s_sem, q_sem, n_sem, o_sem, t_sem,
 ):
     ctx = lax.axis_index("ctx")
@@ -83,15 +86,17 @@
     z_to = [None] + [at((z + d) % NZ, x, y, c) for d in range(1, NZ)]
     x_to = [None] + [at(z, (x + d) % NX, y, c) for d in range(1, NX)]
 
-    wk_copy = pltpu.make_async_copy(wk_hbm, wk, w_sem.at[0])
-    wv_copy = pltpu.make_async_copy(wv_hbm, wv, w_sem.at[1])
-    wk_copy.start()
-    wv_copy.start()
-
     barrier = pltpu.get_barrier_semaphore()
     partners = [ax1p, ax1m, ax2p, ax2m, sib] + z_to[1:] + x_to[1:]
     for who in partners:
         pl.semaphore_signal(barrier, inc=1, device_id=who, device_id_type=MESH)
+    pairs = [(cache_hbm, cache_ref), (q_hbm, q_ref), (new_hbm, new_ref), (wk_hbm, wk), (wv_hbm, wv)]
+    loads = [pltpu.make_async_copy(src, dst, w_sem.at[n]) for n, (src, dst) in enumerate(pairs)]
+    for load in loads:
+        load.start()
+    wk_copy, wv_copy = loads[3:]
+    for load in loads[:3]:
+        load.wait()
 
     length = len_ref[0]
     mine = kbuf.at[0]
@@ -109,15 +114,10 @@
 
     pl.semaphore_wait(barrier, len(partners))
 
-    sent = {}
-
-    def send(key, src, dst, who, recv):
-        number = len(sent)
-        copy = pltpu.make_async_remote_copy(
-            src_ref=src, dst_ref=dst, send_sem=send_sem.at[number], recv_sem=recv, device_id=who, device_id_type=MESH
-        )
-        sent[key] = (number, src)
-        copy.start()
+    def send(kind, src, dst, who, recv):
+        pltpu.make_async_remote_copy(
+            src_ref=src, dst_ref=dst, send_sem=send_sem.at[kind], recv_sem=recv, device_id=who, device_id_type=MESH
+        ).start()
 
     def rows_of(block, half=None):
         ref = kbuf.at[PLACE[block]]
@@ -125,26 +125,23 @@
 
     def k_send(block, to_block, who, half=None):
         _, d1, d2 = to_block
-        key = ("k", to_block, half)
-        send(key, rows_of(block, half), rows_of(to_block, half), who, k_sem.at[d1 * 4 + d2, half or 0])
+        send(0, rows_of(block, half), rows_of(to_block, half), who, k_sem.at[d1 * 4 + d2])
 
     def sib_send(d1, d2):
-        send(("s", d1, d2), rows_of((0, d1, d2)), rows_of((1, d1, d2)), sib, s_sem.at[d1 * 4 + d2])
+        block = (1, d1, d2)
+        send(0, rows_of((0, d1, d2)), rows_of(block), sib, s_sem.at[PLACE[block] // 4])
 
     def wait_at(ref, sem):
         pltpu.make_async_copy(ref, ref, sem).wait()
 
-    def wait_sib(d1, d2):
-        wait_at(rows_of((1, d1, d2)), s_sem.at[d1 * 4 + d2])
+    def wait_sib(chunk):
+        count = sum(b[0] for b in ORDER[4 * chunk : 4 * chunk + 4])
+        if count:
+            wait_at(kbuf.at[4 * chunk : 4 * chunk + count], s_sem.at[chunk])
 
     def event(d1, d2):
         block = (0, d1, d2)
-        sem = d1 * 4 + d2
-        if d2 == 3 or (d1, d2) == (3, 0):
-            wait_at(rows_of(block, 0), k_sem.at[sem, 0])
-            wait_at(rows_of(block, 1), k_sem.at[sem, 1])
-        else:
-            wait_at(rows_of(block), k_sem.at[sem, 0])
+        wait_at(rows_of(block), k_sem.at[d1 * 4 + d2])
         if d2 == 0:
             if d1 == 1:
                 k_send(block, (0, 3, 0), ax1p, 0)
@@ -161,7 +158,7 @@
     def q_send(d, to, half=None, src=None):
         part = slice(0, 192) if half is None else slice(96 * half, 96 * half + 96)
         src = qsend if src is None else src
-        send(("q", d, half), src.at[part], qrecv.at[d, part], to, q_sem.at[d, half or 0])
+        send(1, src.at[part], qrecv.at[d, part], to, q_sem.at[d])
 
     q_send(1, z_to[1])
     q_send(7, z_to[7])
@@ -174,7 +171,7 @@
     k_send(own, (0, 0, 2), ax2m)
     sib_send(0, 0)
     for d in range(1, NX):
-        send(("n", d), nsend, nbuf.at[d], x_to[d], n_sem.at[d])
+        send(2, nsend, nbuf.at[d], x_to[d], n_sem.at[0])
 
     def place(d):
         r = slice(128 * SPOT[d], 128 * SPOT[d] + 128)
@@ -218,8 +215,7 @@
             ktail[BLK * here + 16 * g : BLK * here + 16 * g + 16, :] = jnp.where(lane < 64, piece, bias).astype(bf16)
 
     def mask_new():
-        for d in range(1, NX):
-            wait_at(nbuf.at[d], n_sem.at[d])
+        wait_at(nbuf.at[1:NX], n_sem.at[0])
         n_j = lax.broadcasted_iota(jnp.int32, (16, 128), 0)
         col = lax.broadcasted_iota(jnp.int32, (16, 128), 1) - 64
         q_rank = (col % 8) * (NZ * NX) + (z + NZ - col // 8) % NZ * NX + x
@@ -295,7 +291,7 @@
             total = jnp.sum(tot[r, :], axis=1, keepdims=True)
             ssend[d] = jnp.where(lane == 0, top[r, :], total).T[0:8, :]
             if d:
-                send(("t", d), ssend.at[d], srecv.at[d], z_to[NZ - d], t_sem.at[d])
+                send(3, ssend.at[d], srecv.at[d], z_to[NZ - d], t_sem.at[0])
         for h in range(16):
             rows = pl.ds(HALF * half + h, 32, stride=16)
             part = jnp.concatenate([acc[n, rows, :] for n in range(4)], axis=1)
@@ -306,26 +302,26 @@
         for d in owners:
             if d:
                 osend[d] = ob[128 * SPOT[d] : 128 * SPOT[d] + 128, :].astype(bf16)
-                send(("o", d), osend.at[d], orecv.at[d], z_to[NZ - d], o_sem.at[d])
-
-    def take_near():
-        place(0)
-        wait_at(qrecv.at[2], q_sem.at[2, 0])
+                send(4, osend.at[d], orecv.at[d], z_to[NZ - d], o_sem.at[half])
+
+    def relay():
+        wait_at(qrecv.at[2], q_sem.at[2])
         q_send(3, z_to[1], src=qrecv.at[2])
         q_send(4, z_to[2], half=0, src=qrecv.at[2])
-        wait_at(qrecv.at[6], q_sem.at[6, 0])
+        wait_at(qrecv.at[6], q_sem.at[6])
         q_send(5, z_to[7], src=qrecv.at[6])
         q_send(4, z_to[6], half=1, src=qrecv.at[6])
-        wait_at(qrecv.at[1], q_sem.at[1, 0])
-        wait_at(qrecv.at[7], q_sem.at[7, 0])
-        for d in NEAR[1:]:
+
+    def take_near():
+        wait_at(qrecv.at[1], q_sem.at[1])
+        wait_at(qrecv.at[7], q_sem.at[7])
+        for d in NEAR:
             place(d)
 
     def take_far():
-        wait_at(qrecv.at[3], q_sem.at[3, 0])
-        wait_at(qrecv.at[5], q_sem.at[5, 0])
-        wait_at(qrecv.at[4, 0:96], q_sem.at[4, 0])
-        wait_at(qrecv.at[4, 96:192], q_sem.at[4, 1])
+        wait_at(qrecv.at[3], q_sem.at[3])
+        wait_at(qrecv.at[5], q_sem.at[5])
+        wait_at(qrecv.at[4], q_sem.at[4])
         for d in FAR:
             place(d)
 
@@ -334,12 +330,14 @@
 
     def before(n):
         half, chunk = UNITS[n]
+        if n == 0:
+            relay()
+        for b in PASS.get(n, ()):
+            event(*b)
         if n == 0:
             take_near()
             wk_copy.wait()
             absorb(N)
-        for b in PASS.get(n, ()):
-            event(*b)
         if (half, chunk) == (F, 0):
             take_far()
             absorb(F)
@@ -348,9 +346,8 @@
         if chunk in ready:
             return
         ready.add(chunk)
+        wait_sib(chunk)
         for b in ORDER[4 * chunk : 4 * chunk + 4]:
-            if b[0] == 1:
-                wait_sib(*b[1:])
             unpack(b)
 
     before(0)
@@ -367,8 +364,7 @@
             deliver(F)
     deliver(N)
 
-    for d in range(1, NZ):
-        wait_at(srecv.at[d], t_sem.at[d])
+    wait_at(srecv.at[1:NZ], t_sem.at[0])
     tops = [ssend[0, 0:1, :]] + [srecv[d, 0:1, :] for d in range(1, NZ)]
     totals = [ssend[0, 1:2, :]] + [srecv[d, 1:2, :] for d in range(1, NZ)]
     best = tops[0]
@@ -381,12 +377,14 @@
     shares = [s / full for s in shares]
     by_row = jnp.concatenate(shares + [jnp.zeros((120, 128), f32)], axis=0).T
     result = ob[0:128, :] * by_row[:, 0:1]
+    wait_at(orecv.at[0:4], o_sem.at[F])
     for d in FAR + NEAR[1:]:
-        wait_at(orecv.at[d], o_sem.at[d])
+        if d == NEAR[1]:
+            wait_at(orecv.at[0:3], o_sem.at[N])
         result = result + orecv[d].astype(f32) * by_row[:, d : d + 1]
     out_ref[...] = result.astype(bf16)
-    for number, src in sent.values():
-        pltpu.make_async_copy(src, src, send_sem.at[number]).wait()
+    for kind, ref in enumerate((kbuf.at[0:31], qrecv.at[0:7], nbuf.at[0:3], ssend.at[0:7], osend.at[0:7])):
+        wait_at(ref, send_sem.at[kind])
 
 
 def body(queries, absorb_k, absorb_v, cache, new_entries, cache_len):
@@ -401,9 +399,12 @@
     out = pl.pallas_call(
         run,
         out_shape=jax.ShapeDtypeStruct((128, 128), bf16),
-        in_specs=[vmem, vmem, vmem, pl.BlockSpec(memory_space=pltpu.SMEM), hbm, hbm],
+        in_specs=[hbm, hbm, hbm, pl.BlockSpec(memory_space=pltpu.SMEM), hbm, hbm],
         out_specs=vmem,
         scratch_shapes=[
+            pltpu.VMEM((128, 192), bf16),
+            pltpu.VMEM((576, 128), bf16),
+            pltpu.VMEM((8, 576), bf16),
             pltpu.VMEM((32, PACK, LAT), bf16),
             pltpu.VMEM((32 * BLK, 128), bf16),
             pltpu.VMEM((16, 640), bf16),
@@ -427,14 +428,14 @@
             pltpu.VMEM((NZ, 128, 128), bf16),
             pltpu.VMEM((NZ, 8, 128), f32),
             pltpu.VMEM((NZ, 8, 128), f32),
+            dma((5,)),
+            dma((5,)),
+            dma((16,)),
+            dma((8,)),
+            dma((NZ,)),
+            dma((1,)),
             dma((2,)),
-            dma((88,)),
-            dma((16, 2)),
-            dma((16,)),
-            dma((NZ, 2)),
-            dma((NX,)),
-            dma((NZ,)),
-            dma((NZ,)),
+            dma((1,)),
         ],
         compiler_params=pltpu.CompilerParams(
             collective_id=0, has_side_effects=True, vmem_limit_bytes=56 << 20

time: 49.1 us -> 47 us (0.957)
  Pallas kernels: 46.9 us -> 44.8 us
    pallas_call x1, Pallas kernels: 46.9 us -> 44.8 us  [body(): pl.pallas_call(run, out_shape=jax.ShapeDtypeStruct((128, 128), bf16), in_...]
where the time goes in v3:
time: 47 us; the launch traced here: 46.9 us
  Pallas kernels  44.8 us (95%)
  local copies, waits for them, and re-layouts  1.38 us (3%)
  between operations  0.66 us (1%)
    pallas_call x1, Pallas kernels, body(): pl.pallas_call(run, out_shape=jax.ShapeDtypeStruct((128, 128), bf16), in_...  44.8 us
    unnamed x1, local copies, waits for them, and re-layouts  1.38 us

profile of v3, /device:TPU:1, one launch (start us, length us, event | category | flops | bytes accessed | tf_op | source)
XLA Modules:
  0.0 46.9 jit_solution(12222065600792915036)
XLA Ops:
  0.7 44.8 %shard_map.64 = bf16[128,128]{1,0:T(8,128)(2,1)} custom-call(bf16[128,192]{1,0:T(8,128)(2,1)} %bitcast.5, bf16[576,128]{1,0:T(8,128)(2,1)} %bitcast.3, bf16[8,576]{1,0:T(8,128)(2,1)} %refs_2_.1, s32[1]{0:T(128)S(6)} %copy.8.refs_3_, bf16[16,128,512]{2,1,0:T(8,128)(2,1)} %refs_4_.1, bf16[16,512,128]{2,1,0:T(8,128)(2,1)} %refs_5_.1), custom_call_target="tpu_custom_call" | custom-call | tf_op jit(solution)/shard_map/pallas_call | solution.py:399
  45.5 1.4 %copy.9 = bf16[8,16,128]{2,1,0:T(8,128)(2,1)} copy(bf16[8,16,128]{2,1,0:T(8,128)(2,1)} %bitcast.4) | data formatting | bytes 65536

commit v4 on v3

--- a/solution.py
+++ b/solution.py
@@ -15,7 +15,8 @@
 
 NZ, NX, NY = 8, 4, 4
 BLK = 128
-PACK = 144
+WIDE = 576
+MASK = 64
 LAT = 512
 NEW_ROWS = 64
 CH = 4 * BLK
@@ -66,7 +67,7 @@
 
 def kernel(
     scale, q_hbm, cache_hbm, new_hbm, len_ref, wk_hbm, wv_hbm, out_ref,
-    q_ref, cache_ref, new_ref, kbuf, ktail, nsend, nbuf, qsend, qrecv, qabs, qn, wk, wv, sa, sb, pa, pb, al, top, tot, acc, ob, osend, orecv, ssend, srecv,
+    q_ref, new_ref, kbuf, kbias, nsend, nbuf, newk, qsend, qrecv, qabs, qn, wk, wv, sa, sb, pa, pb, al, top, tot, acc, ob, osend, orecv, ssend, srecv,
     w_sem, send_sem, k_sem, s_sem, q_sem, n_sem, o_sem, t_sem,
 ):
     ctx = lax.axis_index("ctx")
@@ -90,22 +91,17 @@
     partners = [ax1p, ax1m, ax2p, ax2m, sib] + z_to[1:] + x_to[1:]
     for who in partners:
         pl.semaphore_signal(barrier, inc=1, device_id=who, device_id_type=MESH)
-    pairs = [(cache_hbm, cache_ref), (q_hbm, q_ref), (new_hbm, new_ref), (wk_hbm, wk), (wv_hbm, wv)]
+    pairs = [(q_hbm, q_ref), (new_hbm, new_ref), (cache_hbm, kbuf.at[0]), (wk_hbm, wk), (wv_hbm, wv)]
     loads = [pltpu.make_async_copy(src, dst, w_sem.at[n]) for n, (src, dst) in enumerate(pairs)]
     for load in loads:
         load.start()
-    wk_copy, wv_copy = loads[3:]
-    for load in loads[:3]:
+    own_copy, wk_copy, wv_copy = loads[2:]
+    for load in loads[:2]:
         load.wait()
 
     length = len_ref[0]
-    mine = kbuf.at[0]
     qsend[0:128, :] = q_ref[:, 0:128]
     qsend[128:192, :] = jnp.concatenate([q_ref[0:64, 128:192], q_ref[64:128, 128:192]], axis=1)
-    for n in range(4):
-        mine[0:128, 128 * n : 128 * n + 128] = cache_ref[128 * n : 128 * n + 128, :].astype(f32).T.astype(bf16)
-    rope = jnp.concatenate([cache_ref[LAT:576, :].astype(f32), jnp.zeros((64, 128), f32)], axis=0).T
-    mine[128:144, :] = jnp.concatenate([rope[16 * g : 16 * g + 16, 0:64] for g in range(8)], axis=1).astype(bf16)
     fresh = new_ref[...].astype(f32)
     fresh = jnp.concatenate([fresh, jnp.zeros((8, 576), f32)], axis=0)
     fresh = jnp.concatenate([fresh, jnp.zeros((16, 64), f32)], axis=1).astype(bf16)
@@ -121,15 +117,17 @@
 
     def rows_of(block, half=None):
         ref = kbuf.at[PLACE[block]]
-        return ref if half is None else ref.at[0:80] if half == 0 else ref.at[80:144]
-
-    def k_send(block, to_block, who, half=None):
+        return ref if half is None else ref.at[288 * half : 288 * half + 288]
+
+    def k_send(block, to_block, who, half):
         _, d1, d2 = to_block
-        send(0, rows_of(block, half), rows_of(to_block, half), who, k_sem.at[d1 * 4 + d2])
+        src = cache_hbm.at[288 * half : 288 * half + 288] if block == (0, 0, 0) else rows_of(block, half)
+        send(0, src, rows_of(to_block, half), who, k_sem.at[d1 * 4 + d2, half])
 
     def sib_send(d1, d2):
         block = (1, d1, d2)
-        send(0, rows_of((0, d1, d2)), rows_of(block), sib, s_sem.at[PLACE[block] // 4])
+        src = rows_of((0, d1, d2)) if d1 or d2 else cache_hbm
+        send(0, src, rows_of(block), sib, s_sem.at[PLACE[block] // 4])
 
     def wait_at(ref, sem):
         pltpu.make_async_copy(ref, ref, sem).wait()
@@ -139,21 +137,28 @@
         if count:
             wait_at(kbuf.at[4 * chunk : 4 * chunk + count], s_sem.at[chunk])
 
-    def event(d1, d2):
+    def half_event(d1, d2, half):
         block = (0, d1, d2)
-        wait_at(rows_of(block), k_sem.at[d1 * 4 + d2])
+        wait_at(rows_of(block, half), k_sem.at[d1 * 4 + d2, half])
         if d2 == 0:
-            if d1 == 1:
+            if d1 == 1 and half == 0:
                 k_send(block, (0, 3, 0), ax1p, 0)
-            if d1 == 2:
+            if d1 == 2 and half == 1:
                 k_send(block, (0, 3, 0), ax1m, 1)
-            k_send(block, (0, d1, 1), ax2p)
-            k_send(block, (0, d1, 2), ax2m)
-        elif d2 == 1:
+            k_send(block, (0, d1, 1), ax2p, half)
+            k_send(block, (0, d1, 2), ax2m, half)
+        elif d2 == 1 and half == 0:
             k_send(block, (0, d1, 3), ax2p, 0)
-        elif d2 == 2:
+        elif d2 == 2 and half == 1:
             k_send(block, (0, d1, 3), ax2m, 1)
-        sib_send(d1, d2)
+
+    def event(*blocks):
+        for turn in range(2):
+            for d1, d2 in blocks:
+                first = 1 if (d2 or d1) == 2 else 0
+                half_event(d1, d2, first ^ turn)
+        for d1, d2 in blocks:
+            sib_send(d1, d2)
 
     def q_send(d, to, half=None, src=None):
         part = slice(0, 192) if half is None else slice(96 * half, 96 * half + 96)
@@ -165,10 +170,12 @@
     q_send(2, z_to[2])
     q_send(6, z_to[6])
     own = (0, 0, 0)
-    k_send(own, (0, 1, 0), ax1p)
-    k_send(own, (0, 2, 0), ax1m)
-    k_send(own, (0, 0, 1), ax2p)
-    k_send(own, (0, 0, 2), ax2m)
+    for turn in range(2):
+        k_send(own, (0, 1, 0), ax1p, turn)
+        k_send(own, (0, 2, 0), ax1m, 1 - turn)
+    for turn in range(2):
+        k_send(own, (0, 0, 1), ax2p, turn)
+        k_send(own, (0, 0, 2), ax2m, 1 - turn)
     sib_send(0, 0)
     for d in range(1, NX):
         send(2, nsend, nbuf.at[d], x_to[d], n_sem.at[0])
@@ -195,7 +202,7 @@
             for n in range(4):
                 qabs[r, 128 * n : 128 * n + 128] = acc[n, r, :].astype(bf16)
 
-    def unpack(block):
+    def mask_slots(block):
         plane, d1, d2 = block
         first_x = on_x if plane == 0 else on_y
         s1, s2 = OFFSET[d1], OFFSET[d2]
@@ -203,46 +210,39 @@
         sy = (y + s1 * (1 - first_x) + s2 * first_x) % NY
         sc = c if plane == 0 else 1 - c
         slot = ((z * NX + sx) * NY + sy) * (2 * BLK) + sc * BLK
-        here = PLACE[block]
-        packed = kbuf[here, 128:144, :].astype(f32)
-        row = lax.broadcasted_iota(jnp.int32, (16, 128), 0)
-        lane = lax.broadcasted_iota(jnp.int32, (16, 128), 1)
-        for g in range(8):
-            piece = packed[:, 128 * (g // 2) : 128 * (g // 2) + 128]
-            if g % 2:
-                piece = pltpu.roll(piece, 64, 1)
-            bias = jnp.where(slot + 16 * g + row < length, 0.0, NEG)
-            ktail[BLK * here + 16 * g : BLK * here + 16 * g + 16, :] = jnp.where(lane < 64, piece, bias).astype(bf16)
-
-    def mask_new():
+        here = PLACE[block] * BLK
+        key = lax.broadcasted_iota(jnp.int32, (MASK, BLK), 1)
+        kbias[:, here : here + BLK] = jnp.where(slot + key < length, 0.0, NEG).astype(bf16)
+
+    def take_new():
         wait_at(nbuf.at[1:NX], n_sem.at[0])
-        n_j = lax.broadcasted_iota(jnp.int32, (16, 128), 0)
-        col = lax.broadcasted_iota(jnp.int32, (16, 128), 1) - 64
-        q_rank = (col % 8) * (NZ * NX) + (z + NZ - col // 8) % NZ * NX + x
-        for d in range(NX):
-            n_rank = n_j * (NZ * NX) + z * NX + (x + NX - d) % NX
-            bias = jnp.where((n_j < 8) & (n_rank <= q_rank), 0.0, NEG)
-            tail = nbuf[d, :, LAT:640].astype(f32)
-            nbuf[d, :, LAT:640] = jnp.where(col >= 0, bias, tail).astype(bf16)
-
-    def keys_of(chunk, lo):
-        if lo == CH:
-            return jnp.concatenate([nbuf[d] for d in range(NX)], axis=0)
-        b = chunk * 4 + lo // BLK
-        lat = jnp.concatenate([kbuf[b, 0:128, :], kbuf[b + 1, 0:128, :]], axis=0)
-        return jnp.concatenate([lat, ktail[BLK * b : BLK * b + 256, :]], axis=1)
+        rows = [nbuf[d].astype(f32) for d in range(NX)] + [jnp.zeros((NEW_ROWS, 640), f32)]
+        rows = jnp.concatenate(rows, axis=0)
+        for n in range(5):
+            newk[128 * n : 128 * n + 128, :] = rows[:, 128 * n : 128 * n + 128].T.astype(bf16)
+        key = lax.broadcasted_iota(jnp.int32, (MASK, BLK), 1)
+        row = lax.broadcasted_iota(jnp.int32, (MASK, BLK), 0)
+        n_j = key % 16
+        n_rank = n_j * (NZ * NX) + z * NX + (x + NX - key // 16) % NX
+        q_rank = (row % 8) * (NZ * NX) + (z + NZ - row // 8) % NZ * NX + x
+        seen = (key < NEW_ROWS) & (n_j < 8) & (n_rank <= q_rank)
+        newk[WIDE : WIDE + MASK, :] = jnp.where(seen, 0.0, NEG).astype(bf16)
+
+    def keys_of(b):
+        both = jnp.concatenate([kbuf[b], kbuf[b + 1]], axis=1)
+        return jnp.concatenate([both, kbias[:, BLK * b : BLK * b + 2 * BLK]], axis=0)
 
     def scores(unit, s):
         half, chunk = unit
         q = qabs.at[HALF * half : HALF * half + HALF]
         for lo in range(0, CH, 256):
-            s[:, lo : lo + 256] = dot_t(q[...], keys_of(chunk, lo))
+            s[:, lo : lo + 256] = dot_n(q[...], keys_of(4 * chunk + lo // BLK))
         if chunk == 0:
-            s[:, CH : CH + NEW_ROWS] = dot_t(q[...], keys_of(chunk, CH))
+            s[:, CH : CH + BLK] = dot_n(q[...], newk[...])
 
     def weigh(unit, s, p):
         half, chunk = unit
-        size = CH + NEW_ROWS if chunk == 0 else CH
+        size = CH + BLK if chunk == 0 else CH
         for t in range(HALF // 32):
             sr = slice(32 * t, 32 * t + 32)
             r = slice(HALF * half + 32 * t, HALF * half + 32 * t + 32)
@@ -256,10 +256,8 @@
             top[r, :] = new_top
             w = jnp.exp2((sc - new_top[:, 0:1]) * scale)
             part = w[:, 0:128]
-            for lo in range(128, CH, 128):
+            for lo in range(128, size, 128):
                 part = part + w[:, lo : lo + 128]
-            if size > CH:
-                part = part + jnp.concatenate([w[:, CH:size], jnp.zeros((32, 128 - NEW_ROWS), f32)], axis=1)
             if chunk:
                 part = part + tot[r, :] * shrink
             tot[r, :] = part
@@ -267,17 +265,17 @@
 
     def mix(unit, p):
         half, chunk = unit
-        size = CH + NEW_ROWS if chunk == 0 else CH
+        size = CH + BLK if chunk == 0 else CH
         for n in range(2):
             cols = slice(256 * n, 256 * n + 256)
-            v = [kbuf[chunk * 4 + b, 0:128, cols] for b in range(4)]
+            v = [kbuf[chunk * 4 + b, cols, :] for b in range(4)]
             if chunk == 0:
-                v = v + [nbuf[d, :, cols] for d in range(NX)]
-            v = jnp.concatenate(v, axis=0)
+                v = v + [newk[cols, :]]
+            v = jnp.concatenate(v, axis=1)
             for t in range(HALF // 256):
                 sr = slice(256 * t, 256 * t + 256)
                 r = slice(HALF * half + 256 * t, HALF * half + 256 * t + 256)
-                o = dot_n(p[sr, 0:size], v)
+                o = dot_t(p[sr, 0:size], v)
                 for k in range(2):
                     part = o[:, 128 * k : 128 * k + 128]
                     m = 2 * n + k
@@ -332,8 +330,7 @@
         half, chunk = UNITS[n]
         if n == 0:
             relay()
-        for b in PASS.get(n, ()):
-            event(*b)
+        event(*PASS.get(n, ()))
         if n == 0:
             take_near()
             wk_copy.wait()
@@ -342,13 +339,14 @@
             take_far()
             absorb(F)
         if n == 0:
-            mask_new()
+            take_new()
+            own_copy.wait()
         if chunk in ready:
             return
         ready.add(chunk)
         wait_sib(chunk)
         for b in ORDER[4 * chunk : 4 * chunk + 4]:
-            unpack(b)
+            mask_slots(b)
 
     before(0)
     scores(UNITS[0], sa)
@@ -403,12 +401,12 @@
         out_specs=vmem,
         scratch_shapes=[
             pltpu.VMEM((128, 192), bf16),
-            pltpu.VMEM((576, 128), bf16),
             pltpu.VMEM((8, 576), bf16),
-            pltpu.VMEM((32, PACK, LAT), bf16),
-            pltpu.VMEM((32 * BLK, 128), bf16),
+            pltpu.VMEM((32, WIDE, BLK), bf16),
+            pltpu.VMEM((MASK, 32 * BLK), bf16),
             pltpu.VMEM((16, 640), bf16),
             pltpu.VMEM((NX, 16, 640), bf16),
+            pltpu.VMEM((640, BLK), bf16),
             pltpu.VMEM((192, 128), bf16),
             pltpu.VMEM((NZ, 192, 128), bf16),
             pltpu.VMEM((ROWS, 640), bf16),
@@ -430,7 +428,7 @@
             pltpu.VMEM((NZ, 8, 128), f32),
             dma((5,)),
             dma((5,)),
-            dma((16,)),
+            dma((16, 2)),
             dma((8,)),
             dma((NZ,)),
             dma((1,)),

time: 47 us -> 45.6 us (0.970)
  Pallas kernels: 44.8 us -> 43.4 us
    pallas_call x1, Pallas kernels: 44.8 us -> 43.4 us  [body(): pl.pallas_call(run, out_shape=jax.ShapeDtypeStruct((128, 128), bf16), in_...]
where the time goes in v4:
time: 45.6 us; the launch traced here: 45.5 us
  Pallas kernels  43.4 us (95%)
  local copies, waits for them, and re-layouts  1.38 us (3%)
  between operations  0.66 us (1%)
    pallas_call x1, Pallas kernels, body(): pl.pallas_call(run, out_shape=jax.ShapeDtypeStruct((128, 128), bf16), in_...  43.4 us
    unnamed x1, local copies, waits for them, and re-layouts  1.38 us

profile of v4, /device:TPU:1, one launch (start us, length us, event | category | flops | bytes accessed | tf_op | source)
XLA Modules:
  0.0 45.5 jit_solution(2266272461788362887)
XLA Ops:
  0.7 43.4 %shard_map.64 = bf16[128,128]{1,0:T(8,128)(2,1)} custom-call(bf16[128,192]{1,0:T(8,128)(2,1)} %bitcast.5, bf16[576,128]{1,0:T(8,128)(2,1)} %bitcast.3, bf16[8,576]{1,0:T(8,128)(2,1)} %refs_2_.1, s32[1]{0:T(128)S(6)} %copy.8.refs_3_, bf16[16,128,512]{2,1,0:T(8,128)(2,1)} %refs_4_.1, bf16[16,512,128]{2,1,0:T(8,128)(2,1)} %refs_5_.1), custom_call_target="tpu_custom_call" | custom-call | tf_op jit(solution)/shard_map/pallas_call | solution.py:397
  44.1 1.4 %copy.9 = bf16[8,16,128]{2,1,0:T(8,128)(2,1)} copy(bf16[8,16,128]{2,1,0:T(8,128)(2,1)} %bitcast.4) | data formatting | bytes 65536

commit v5 on v4

--- a/solution.py
+++ b/solution.py
@@ -45,16 +45,7 @@
     (N, 0), (N, 1), (F, 0), (F, 1), (N, 2), (F, 2), (F, 3), (F, 4),
     (F, 5), (F, 6), (F, 7), (N, 3), (N, 4), (N, 5), (N, 6), (N, 7),
 ]
-PASS = {
-    0: [(1, 0), (2, 0), (0, 1), (0, 2)],
-    2: [(3, 0), (0, 3)],
-    3: [(1, 1), (1, 2)],
-    4: [(2, 1), (2, 2)],
-    5: [(3, 1)],
-    6: [(3, 2), (1, 3)],
-    7: [(2, 3)],
-    8: [(3, 3)],
-}
+PASS = {0: [(1, 0), (2, 0)], 1: [(0, 1), (0, 2)], 2: [(3, 0)], 3: [(1, 1), (1, 2), (0, 3)], 4: [(2, 1), (2, 2)], 5: [(3, 1), (3, 2)], 7: [(1, 3), (2, 3)], 8: [(3, 3)]}
 
 
 def dot_t(a, b):
@@ -88,7 +79,7 @@
     x_to = [None] + [at(z, (x + d) % NX, y, c) for d in range(1, NX)]
 
     barrier = pltpu.get_barrier_semaphore()
-    partners = [ax1p, ax1m, ax2p, ax2m, sib] + z_to[1:] + x_to[1:]
+    partners = [ax1p, ax1m, ax2p, ax2m, sib, x_to[2]] + z_to[1:]
     for who in partners:
         pl.semaphore_signal(barrier, inc=1, device_id=who, device_id_type=MESH)
     pairs = [(q_hbm, q_ref), (new_hbm, new_ref), (cache_hbm, kbuf.at[0]), (wk_hbm, wk), (wv_hbm, wv)]
@@ -165,6 +156,8 @@
         src = qsend if src is None else src
         send(1, src.at[part], qrecv.at[d, part], to, q_sem.at[d])
 
+    for d in range(1, NX):
+        send(2, nsend, nbuf.at[d], x_to[d], n_sem.at[0])
     q_send(1, z_to[1])
     q_send(7, z_to[7])
     q_send(2, z_to[2])
@@ -177,8 +170,6 @@
         k_send(own, (0, 0, 1), ax2p, turn)
         k_send(own, (0, 0, 2), ax2m, 1 - turn)
     sib_send(0, 0)
-    for d in range(1, NX):
-        send(2, nsend, nbuf.at[d], x_to[d], n_sem.at[0])
 
     def place(d):
         r = slice(128 * SPOT[d], 128 * SPOT[d] + 128)
@@ -313,7 +304,7 @@
     def take_near():
         wait_at(qrecv.at[1], q_sem.at[1])
         wait_at(qrecv.at[7], q_sem.at[7])
-        for d in NEAR:
+        for d in NEAR[1:]:
             place(d)
 
     def take_far():
@@ -339,15 +330,16 @@
             take_far()
             absorb(F)
         if n == 0:
-            take_new()
             own_copy.wait()
         if chunk in ready:
             return
         ready.add(chunk)
         wait_sib(chunk)
-        for b in ORDER[4 * chunk : 4 * chunk + 4]:
-            mask_slots(b)
-
+
+    place(0)
+    for b in ORDER:
+        mask_slots(b)
+    take_new()
     before(0)
     scores(UNITS[0], sa)
     for n, unit in enumerate(UNITS):

time: 45.6 us -> 45.5 us (level)
  no operation moved by 1% of the time
where the time goes in v5:
time: 45.5 us; the launch traced here: 45.3 us
  Pallas kernels  43.3 us (95%)
  local copies, waits for them, and re-layouts  1.38 us (3%)
  between operations  0.66 us (1%)
    pallas_call x1, Pallas kernels, body(): pl.pallas_call(run, out_shape=jax.ShapeDtypeStruct((128, 128), bf16), in_...  43.3 us
    unnamed x1, local copies, waits for them, and re-layouts  1.38 us

profile of v5, /device:TPU:1, one launch (start us, length us, event | category | flops | bytes accessed | tf_op | source)
XLA Modules:
  0.0 45.3 jit_solution(14479279812271621670)
XLA Ops:
  0.7 43.3 %shard_map.64 = bf16[128,128]{1,0:T(8,128)(2,1)} custom-call(bf16[128,192]{1,0:T(8,128)(2,1)} %bitcast.5, bf16[576,128]{1,0:T(8,128)(2,1)} %bitcast.3, bf16[8,576]{1,0:T(8,128)(2,1)} %refs_2_.1, s32[1]{0:T(128)S(6)} %copy.8.refs_3_, bf16[16,128,512]{2,1,0:T(8,128)(2,1)} %refs_4_.1, bf16[16,512,128]{2,1,0:T(8,128)(2,1)} %refs_5_.1), custom_call_target="tpu_custom_call" | custom-call | tf_op jit(solution)/shard_map/pallas_call | solution.py:389
  43.9 1.4 %copy.9 = bf16[8,16,128]{2,1,0:T(8,128)(2,1)} copy(bf16[8,16,128]{2,1,0:T(8,128)(2,1)} %bitcast.4) | data formatting | bytes 65536
